TPU v7x, 128 devices: a whole 4x4x4 slice. The times are simulated.
128 devices in a mesh: shard: 16 (over z, y_hi, core), replica: 8 (over x, y_lo).
Axes of the slice: x: 4, y: 4 (y_hi: 2, y_lo: 2; y = y_hi * 2 + y_lo), z: 4, core: 2. Of those that a mesh axis runs over, the one named last changes fastest.
Arguments:
- tokens: bfloat16 [4096, 3072], P('replica'), may hold values from -6 to 6
- target: bfloat16 [4096, 3072], P('replica'), may hold values from -6 to 6
- w_in: bfloat16 [3072, 12288], P('replica', 'shard'), may hold values from -0.109375 to 0.109375
- probe_in: bfloat16 [3072, 12288], P('replica', 'shard'), may hold values from -1.5 to 1.5
- w_out: bfloat16 [3072, 12288], P('replica', 'shard'), may hold values from -0.0546875 to 0.0546875
- probe_out: bfloat16 [3072, 12288], P('replica', 'shard'), may hold values from -6 to 6
Outputs:
- grad_in: float32 [3072, 12288], P('replica', 'shard')
- hess_in: float32 [3072, 12288], P('replica', 'shard')
- grad_out: float32 [3072, 12288], P('replica', 'shard')
- hess_out: float32 [3072, 12288], P('replica', 'shard')
All inputs are finite; a program needn't handle non-finite values.
Results may differ from a plain program's by a relative error of at most 0.025.
Values may be sent and summed in bfloat16 or wider, within the bound.
A program may use at most 192 MiB of HBM per device.

v0:
```python
import jax
import jax.numpy as jnp
from jax import lax
from jax.sharding import PartitionSpec as P


def dot_f32(left, right):
    return jnp.dot(left, right, preferred_element_type=jnp.float32)


def inner_rows(left, right):
    return lax.dot_general(
        left, right, (((0,), (0,)), ((), ())), preferred_element_type=jnp.float32
    )


def outer_rows(left, right):
    return lax.dot_general(
        left, right, (((1,), (1,)), ((), ())), preferred_element_type=jnp.float32
    )


def error_pair(out_part, dot_part, target_rows, loss_scale):
    output, out_dot = (
        lax.psum(out_part.astype(jnp.bfloat16), "shard").astype(jnp.float32),
        lax.psum(dot_part.astype(jnp.bfloat16), "shard").astype(jnp.float32),
    )
    error_term = (loss_scale * (output - target_rows.astype(jnp.float32))).astype(jnp.bfloat16)
    error_dot = (loss_scale * out_dot).astype(jnp.bfloat16)
    return (error_term, error_dot)


def on_device(tokens, target, w_in, probe_in, w_out, probe_out):
    hid_local = w_in.shape[1]
    tok_local = tokens.shape[0]
    groups = lax.axis_size("replica")
    total_tokens = tok_local * groups
    loss_scale = float(total_tokens) ** (-0.5)
    stacked = jnp.concatenate(
        (
            lax.all_gather(w_in, "replica", axis=0, tiled=True),
            lax.all_gather(probe_in, "replica", axis=0, tiled=True),
        ),
        1,
    )
    columns = tokens
    pre_both = dot_f32(columns, stacked)
    hidden_pre = pre_both[:, :hid_local]
    pre_dot = pre_both[:, hid_local:]
    normal_cdf = 0.5 * (1.0 + jax.scipy.special.erf(hidden_pre * 0.7071067811865476))
    density = jnp.exp(-0.5 * hidden_pre * hidden_pre) * 0.3989422804014327
    first_deriv = normal_cdf + hidden_pre * density
    curve_term = density * (2.0 - hidden_pre * hidden_pre)
    activation = (hidden_pre * normal_cdf).astype(jnp.bfloat16)
    act_dot = (first_deriv * pre_dot).astype(jnp.bfloat16)
    full_out, full_probe = (
        lax.all_gather(w_out, "replica", axis=0, tiled=True),
        lax.all_gather(probe_out, "replica", axis=0, tiled=True),
    )
    full_pair = jnp.concatenate((full_out, full_probe), 1)
    out_part = outer_rows(activation, full_out)
    dot_part = outer_rows(jnp.concatenate((act_dot, activation), 1), full_pair)
    error_term, error_dot = error_pair(out_part, dot_part, target, loss_scale)
    act_pair = jnp.concatenate((activation, act_dot), 1)
    paired_rows = inner_rows(error_term, act_pair)
    tangent_rows = inner_rows(error_dot, activation)
    out_summed = lax.psum_scatter(
        jnp.concatenate(
            (paired_rows[:, :hid_local], paired_rows[:, hid_local:] + tangent_rows), 1
        ).astype(jnp.bfloat16),
        "replica",
        scatter_dimension=0,
        tiled=True,
    ).astype(jnp.float32)
    grad_out = out_summed[:, :hid_local]
    hv_out = out_summed[:, hid_local:]
    back_pair = dot_f32(error_term, full_pair)
    back_grad = back_pair[:, :hid_local]
    back_dot = dot_f32(error_dot, full_out) + back_pair[:, hid_local:]
    hess_out = loss_scale * probe_out.astype(jnp.float32) * hv_out
    pre_grad = (back_grad * first_deriv).astype(jnp.bfloat16)
    pre_grad_dot = (back_dot * first_deriv + back_grad * curve_term * pre_dot).astype(jnp.bfloat16)
    grad_pair = jnp.concatenate((pre_grad, pre_grad_dot), 1)
    columns = tokens
    in_summed = lax.psum_scatter(
        inner_rows(columns, grad_pair).astype(jnp.bfloat16),
        "replica",
        scatter_dimension=0,
        tiled=True,
    ).astype(jnp.float32)
    grad_in = in_summed[:, :hid_local]
    hess_in = loss_scale * probe_in.astype(jnp.float32) * in_summed[:, hid_local:]
    return (grad_in, hess_in, grad_out, hess_out)


def solution(mesh):
    return jax.shard_map(
        on_device,
        mesh=mesh,
        in_specs=(
            P("replica", None),
            P("replica", None),
            P("replica", "shard"),
            P("replica", "shard"),
            P("replica", "shard"),
            P("replica", "shard"),
        ),
        out_specs=(
            P("replica", "shard"),
            P("replica", "shard"),
            P("replica", "shard"),
            P("replica", "shard"),
        ),
        check_vma=False,
    )
```

profile of v0, /device:TPU:1, one launch (start us, length us, event | category | flops | bytes accessed | tf_op | source)
XLA Modules:
  0.0 1054.4 jit_solution(10492623310781402285)
XLA Ops:
  10.0 102.4 %all-gather.7.cloned.1.call-done = bf16[3072,768]{1,0:T(8,128)(2,1)} async-done(((bf16[384,768]{1,0:T(8,128)(2,1)}), bf16[3072,768]{1,0:T(8,128)(2,1)}) %all-gather.7.cloned.1.call-update) | async-done | bytes 4718608 | tf_op jit(solution)/shard_map/all_gather | solution.py:42
  112.4 102.2 %all-gather.5.cloned.1.call-done = bf16[3072,768]{1,0:T(8,128)(2,1)} async-done(((bf16[384,768]{1,0:T(8,128)(2,1)}), bf16[3072,768]{1,0:T(8,128)(2,1)}) %all-gather.5.cloned.1.call-update) | async-done | bytes 4718608 | tf_op jit(solution)/shard_map/all_gather | solution.py:41
  214.6 9.0 fusion.6
  227.8 89.0 %all-gather.9.cloned.1.call-done = bf16[3072,768]{1,0:T(8,128)(2,1)} async-done(((bf16[384,768]{1,0:T(8,128)(2,1)}), bf16[3072,768]{1,0:T(8,128)(2,1)}) %all-gather.9.cloned.1.call-update) | async-done | bytes 4718608 | tf_op jit(solution)/shard_map/all_gather | solution.py:57
  316.8 4.9 constant_dynamic-update-slice_fusion.1
  321.7 97.2 %all-gather.11.cloned.1.call-done = bf16[3072,768]{1,0:T(8,128)(2,1)} async-done(((bf16[384,768]{1,0:T(8,128)(2,1)}), bf16[3072,768]{1,0:T(8,128)(2,1)}) %all-gather.11.cloned.1.call-update) | async-done | bytes 4718608 | tf_op jit(solution)/shard_map/all_gather | solution.py:58
  418.8 5.2 constant_dynamic-update-slice_fusion
  424.0 10.4 convolution_convert_fusion.1
  434.4 4.1 convolution_convert_fusion.2
  438.8 168.5 %all-reduce.3.cloned.1.call-done = (bf16[512,3072]{1,0:T(8,128)(2,1)}, bf16[512,3072]{1,0:T(8,128)(2,1)}) async-done(((bf16[512,3072]{1,0:T(8,128)(2,1)}, bf16[512,3072]{1,0:T(8,128)(2,1)}), (bf16[512,3072]{1,0:T(8,128)(2,1)}, bf16[512,3072]{1,0:T(8,128)(2,1)})) %all-reduce.3.cloned.1.call-update) | async-done | bytes 6291472 | tf_op jit(solution)/shard_map/psum | solution.py:25
  607.2 9.7 fusion.30
  618.9 5.6 fusion.18
  624.5 8.6 fusion
  633.1 12.6 %copy.27 = bf16[3072,1536]{1,0:T(8,128)(2,1)} copy(bf16[3072,1536]{0,1:T(8,128)(2,1)} %fusion) | data formatting | bytes 18874368
  647.1 12.9 %fusion.26 = f32[3072,1536]{0,1:T(8,128)} fusion(bf16[512,768]{0,1:T(8,128)(2,1)S(1)} %copy-done.12, bf16[512,768]{0,1:T(8,128)(2,1)S(1)} %copy-done.10, bf16[512,3072]{1,0:T(8,128)(2,1)} %param.7, bf16[512,3072]{1,0:T(8,128)(2,1)} %get-tuple-element.12), kind=kOutput, calls=%fused_computation.34 | convolution fusion | flops 4842848256 | bytes 26738688 | tf_op jit(solution)/shard_map/dot_general | solution.py:12
  660.0 4.5 slice.76
  664.5 5.2 fusion.1
  669.7 4.4 pad_maximum_fusion
  674.1 12.7 %copy.29 = bf16[3072,1536]{1,0:T(8,128)(2,1)} copy(bf16[3072,1536]{0,1:T(8,128)(2,1)} %pad_maximum_fusion) | data formatting | bytes 18874368
  689.3 147.0 %reduce-scatter.7.cloned.1.call-done = bf16[384,1536]{1,0:T(8,128)(2,1)} async-done(((bf16[3072,1536]{1,0:T(8,128)(2,1)}), bf16[384,1536]{1,0:T(8,128)(2,1)}) %reduce-scatter.7.cloned.1.call-update) | async-done | bytes 1179664
  840.7 188.0 %reduce-scatter.9.cloned.1.call-done = bf16[384,1536]{1,0:T(8,128)(2,1)} async-done(((bf16[3072,1536]{1,0:T(8,128)(2,1)}), bf16[384,1536]{1,0:T(8,128)(2,1)}) %reduce-scatter.9.cloned.1.call-update) | async-done | bytes 1179664
  1033.0 2.8 copy.22
  1039.6 2.8 copy.24
  1044.9 2.7 copy.25
  (63 shorter events, 28.0 us)
Async XLA Ops:
  7.2 207.4 %copy-start = (bf16[512,3072]{1,0:T(8,128)(2,1)S(1)}, bf16[512,3072]{1,0:T(8,128)(2,1)}, u32[]{:S(2)}) copy-start(bf16[512,3072]{1,0:T(8,128)(2,1)} %param.6) | copy-start | bytes 9437188
  7.2 105.2 %all-gather.7.cloned.1.call-start = ((), (), s32[]{:S(2)}) async-start(), calls=%async_computation.3 | async-start | bytes 5308416 | tf_op jit(solution)/shard_map/all_gather | solution.py:42
  7.9 206.7 %all-gather.5.cloned.1.call-start = ((), (), s32[]{:S(2)}) async-start(), calls=%async_computation.2 | async-start | bytes 5308416 | tf_op jit(solution)/shard_map/all_gather | solution.py:41
  8.7 308.1 %all-gather.9.cloned.1.call-start = ((), (), s32[]{:S(2)}) async-start(), calls=%async_computation.4 | async-start | bytes 5308416 | tf_op jit(solution)/shard_map/all_gather | solution.py:57
  9.4 409.4 %all-gather.11.cloned.1.call-start = ((), (), s32[]{:S(2)}) async-start(), calls=%async_computation.5 | async-start | bytes 5308416 | tf_op jit(solution)/shard_map/all_gather | solution.py:58
  10.0 597.3 %all-reduce.3.cloned.1.call-start = ((), (), s32[]{:S(2)}) async-start(), calls=%async_computation.8 | async-start | bytes 12582912 | tf_op jit(solution)/shard_map/psum | solution.py:25
  223.6 1.9 copy-start.4
  225.5 1.2 copy-start.2
  418.8 5.2 copy-start.9
  418.8 5.2 copy-start.11
  418.8 15.6 %slice-start = ((s8[4718592]{0:T(1024)(128)(4,1)}), s8[4194304]{0:T(1024)(128)(4,1)S(1)}, s32[]{:S(2)}) async-start(s8[4718592]{0:T(1024)(128)(4,1)} %bitcast.14), calls=%async_computation.9 | async-start | bytes 8388608
  424.0 10.4 slice-start.1
  438.5 397.8 %reduce-scatter.7.cloned.1.call-start = ((), (), s32[]{:S(2)}) async-start(), calls=%async_computation.6 | async-start | bytes 10616832
  607.2 9.8 copy-start.3
  607.2 9.8 copy-start.5
  617.0 1.9 copy-start.13
  645.7 1.1 copy-start.10
  645.7 1.4 copy-start.12
  645.7 382.9 %reduce-scatter.9.cloned.1.call-start = ((), (), s32[]{:S(2)}) async-start(), calls=%async_computation.7 | async-start | bytes 10616832
  660.0 4.6 copy-start.14
  686.8 1.1 copy-start.7
  686.8 1.4 copy-start.8
  1033.0 2.8 copy-start.6
  1039.6 8.0 copy-start.1
Sparse Core Ops, SparseCore 0:
  9.7 102.7 all-gather.6
  114.1 100.4 all-gather.4
  216.3 100.4 all-gather.8
  318.3 100.4 all-gather.10
  438.7 168.5 all-reduce.2
  645.9 190.4 reduce-scatter.6
  838.7 189.8 reduce-scatter.8
where the time goes:
time: 1060 us; the launch traced here: 1050 us
  waiting for transfers between devices  897 us (85%)
  matrix products  65.5 us (6%)
  local copies, waits for them, and re-layouts  62.4 us (6%)
  other arithmetic  14.8 us (1%)
  between operations  14.3 us (1%)
    unnamed x9, waiting for transfers between devices  338 us
    psum x1, waiting for transfers between devices, error_pair(): lax.psum(out_part.astype(jnp.bfloat16), 'shard').astype(jnp.float32)  168 us
    all_gather x1, waiting for transfers between devices, on_device(): lax.all_gather(probe_in, 'replica', axis=0, tiled=True)  102 us
    all_gather x1, waiting for transfers between devices, on_device(): lax.all_gather(w_in, 'replica', axis=0, tiled=True)  102 us
    all_gather x1, waiting for transfers between devices, on_device(): lax.all_gather(probe_out, 'replica', axis=0, tiled=True)  97.2 us
    all_gather x1, waiting for transfers between devices, on_device(): lax.all_gather(w_out, 'replica', axis=0, tiled=True)  89 us
    unnamed x45, local copies, waits for them, and re-layouts  50.5 us
    dot_general x3, matrix products, inner_rows(): lax.dot_general(left, right, (((0,), (0,)), ((), ())), preferred_element_...  26.6 us
  transfers between devices with their start and end apart: 7, of which 7 were waited for; matrix products, arithmetic and copies ran while one was open for 6% of the time, Pallas kernels for 0%

commit v1 on v0

v1 whole, which is shorter than its diff:
```python
import functools

import jax
import jax.numpy as jnp
from jax import lax
from jax.experimental import pallas as pl
from jax.experimental.pallas import tpu as pltpu
from jax.sharding import PartitionSpec as P

MESH = pl.DeviceIdType.MESH
BF, F32 = jnp.bfloat16, jnp.float32
N_SEM = 160


def dot_nn(a, b):
    return jnp.dot(a, b, preferred_element_type=F32)


def dot_nt(a, b):
    return lax.dot_general(a, b, (((1,), (1,)), ((), ())), preferred_element_type=F32)


def dot_tn(a, b):
    return lax.dot_general(a, b, (((0,), (0,)), ((), ())), preferred_element_type=F32)


def block_kernel(
    scale, tok, tgt, w_in, p_in, w_out, p_out, out,
    Tk, Wi, Wo, acc, ad, fg, snd, sm, fr, fv, s2, sr, sv, err, xr, xv, ys, stage, tg, lsem, ssem, rsem,
):
    R = w_in.shape[0]
    H = w_in.shape[1] // 2
    T = tok.shape[0]
    K = 2 * R
    C = 2 * H

    shard, rep = lax.axis_index("shard"), lax.axis_index("replica")
    z, yh, c = shard // 4, (shard // 2) % 2, shard % 2
    x, l = rep // 2, rep % 2
    y = yh * 2 + l
    d = 1 - c

    def dev(x_, y_, z_, c_):
        x_, y_, z_ = x_ % 4, y_ % 4, z_ % 4
        return {"shard": z_ * 4 + (y_ // 2) * 2 + c_, "replica": x_ * 2 + y_ % 2}

    xp, xm = dev(x + 1, y, z, c), dev(x + 3, y, z, c)
    yp, ym = dev(x, y + 1, z, c), dev(x, y + 3, z, c)
    zp, zm = dev(x, y, z + 1, c), dev(x, y, z + 3, c)
    core = dev(x, y, z, d)
    mate = dev(x, yh * 2 + 1 - l, z, c)
    fp, fm = dev(x, y + c, z + d, c), dev(x, y + 3 * c, z + 3 * d, c)
    sp, sn = dev(x, y + d, z + c, c), dev(x, y + 3 * d, z + 3 * c, c)
    f, s = d * z + c * y, d * y + c * z

    barrier = pltpu.get_barrier_semaphore()
    for n in (xp, xm, yp, ym, zp, zm, core):
        pl.semaphore_signal(barrier, inc=1, device_id=n, device_id_type=MESH)
    pl.semaphore_wait(barrier, 7)

    ids = {}

    def copy(name, src, dst, to):
        n = ids.setdefault(name, len(ids))
        assert n < N_SEM
        cp = pltpu.make_async_remote_copy(
            src_ref=src, dst_ref=dst, send_sem=ssem.at[n], recv_sem=rsem.at[n], device_id=to, device_id_type=MESH
        )
        cp.start()
        return cp

    pending = []

    def send(name, src, dst, to):
        cp = copy(name, src, dst, to)
        pending.append(cp)
        return cp

    def al(v, m):
        return pl.multiple_of(v, m)

    def rows(i, n):
        return pl.ds(al(i * n, n), n)

    A, B = pl.ds(0, H), pl.ds(H, H)
    L, M = pl.ds(0, K), pl.ds(K, K)
    own, oth = rows(x * 2 + l, R), rows(x * 2 + 1 - l, R)

    def wrow(kx, lo):
        return rows((kx % 4) * 2 + lo, R)

    mine, theirs = rows(l, H), rows(1 - l, H)
    loc = []

    def local(src, dst):
        cp = pltpu.make_async_copy(src, dst, lsem.at[len(loc)])
        cp.start()
        loc.append(cp)
        return cp

    wi_loc = [local(w_in.at[:, mine], Wi.at[own, A]), local(p_in.at[:, mine], Wi.at[own, B])]
    yin = [send("yi0", w_in.at[:, theirs], Wi.at[own, A], mate), send("yi1", p_in.at[:, theirs], Wi.at[own, B], mate)]
    Q = T // 4
    tk = []
    for j, to in ((0, yp), (1, ym)):
        r = rows(2 * j + c, Q)
        tk.append(send("tk%d" % j, tok.at[r], Tk.at[pl.ds(al(l * T + (2 * j + c) * Q, Q), Q)], to))
    wo_loc = [local(w_out.at[:, mine], Wo.at[own, A]), local(p_out.at[:, mine], Wo.at[own, B])]
    tk_loc = local(tok, Tk.at[rows(l, T)])
    G = T // 16
    tg_loc = local(tgt.at[pl.ds(al(f * 4 * G + s * G, G), G)], tg.at[0])
    ym_ = yh * 2 + 1 - l
    f_, s_ = d * z + c * ym_, d * ym_ + c * z
    tgx = send("tg", tgt.at[pl.ds(al(f_ * 4 * G + s_ * G, G), G)], tg.at[1], mate)

    def ring1(tag, W, rws):
        return [send(tag + "p", W.at[rws], W.at[rws], xp), send(tag + "m", W.at[rws], W.at[rws], xm)]

    def ring2(tag, W, lo):
        a, b = wrow(x + 3, lo), wrow(x + 1, lo)
        return [send(tag + "p", W.at[a, A], W.at[a, A], xp), send(tag + "m", W.at[b, B], W.at[b, B], xm)]

    def got(cps):
        for cp in cps:
            cp.wait_recv()

    for cp in wi_loc:
        cp.wait()
    i1o = ring1("i1o", Wi, own)
    got(yin)
    i1t = ring1("i1t", Wi, oth)
    yout = [send("yo0", w_out.at[:, theirs], Wo.at[own, A], mate), send("yo1", p_out.at[:, theirs], Wo.at[own, B], mate)]
    got(i1o)
    i2o = ring2("i2o", Wi, l)
    got(tk)
    tc = []
    for j in (0, 1):
        r = pl.ds(al((1 - l) * T + (2 * j + c) * Q, Q), Q)
        tc.append(send("tc%d" % j, Tk.at[r], Tk.at[r], core))
    got(i1t)
    i2t = ring2("i2t", Wi, 1 - l)
    for cp in wo_loc:
        cp.wait()
    o1o = ring1("o1o", Wo, own)
    got(tc)
    tk_loc.wait()

    def pre_tile(r, kx):
        col = rows(kx % 4, K)
        return dot_nn(Tk[r, col], Wi[col, :])

    def pre_chunk(kx, first):
        @pl.loop(0, 4)
        def _(i):
            r = rows(i, 256)
            v = pre_tile(r, kx)
            acc[r, :] = v if first else acc[r, :] + v

    pre_chunk(x, True)
    got(yout)
    o1t = ring1("o1t", Wo, oth)
    pre_chunk(x + 1, False)
    pre_chunk(x + 3, False)
    got(i2o)
    got(i2t)

    @pl.loop(0, 8)
    def _(i):
        r = rows(i, 128)
        v = acc[r, :] + pre_tile(r, x + 2)
        h, pd = v[:, :H], v[:, H:]
        cdf = 0.5 * (1.0 + lax.erf(h * 0.7071067811865476))
        den = jnp.exp(-0.5 * h * h) * 0.3989422804014327
        fd = cdf + h * den
        ad[r, A] = (fd * pd).astype(BF)
        ad[r, B] = (h * cdf).astype(BF)
        fg[r, A] = fd
        fg[r, B] = den * (2.0 - h * h) * pd

    chunk = [x, x + 1, x + 3, x + 2]
    st = [dict() for _ in range(4)]

    def out_tile(i, r):
        w = rows(chunk[i] % 4, K)
        o = dot_nt(ad[r, B], Wo[w, A])
        t = dot_nt(ad[r, :], Wo[w, :])
        return o, t

    def sA(i):
        slot = i % 2
        if i >= 2:
            st[i - 2]["core"].wait_send()

        @pl.loop(0, T // 256)
        def _(j):
            o, t = out_tile(i, pl.ds(al(d * T + j * 256, 256), 256))
            snd[slot, rows(j, 256), L] = o.astype(BF)
            snd[slot, rows(j, 256), M] = t.astype(BF)

        st[i]["core"] = copy("ca%d" % i, snd.at[slot], sm.at[i], core)

    def sB(i):
        st[i]["core"].wait_recv()

        @pl.loop(0, T // 256)
        def _(j):
            o, t = out_tile(i, pl.ds(al(c * T + j * 256, 256), 256))
            r = rows(j, 256)
            sm[i, r, L] = (o + sm[i, r, L].astype(F32)).astype(BF)
            sm[i, r, M] = (t + sm[i, r, M].astype(F32)).astype(BF)

        r = rows((f + 2) % 4, 4 * G)
        st[i]["f1"] = [
            copy("fp%d" % i, sm.at[i, r, L], fr.at[i, 0], fp),
            copy("fm%d" % i, sm.at[i, r, M], fr.at[i, 1], fm),
        ]

    def add_to(buf, i, r, col, other):
        buf[i, r, col] = (buf[i, r, col].astype(F32) + other.astype(F32)).astype(BF)

    def sC(i):
        got(st[i]["f1"])
        rp, rm = rows((f + 1) % 4, 4 * G), rows((f + 3) % 4, 4 * G)
        add_to(sm, i, rp, L, fr[i, 0])
        add_to(sm, i, rm, M, fr[i, 1])
        st[i]["f2"] = [
            copy("gp%d" % i, sm.at[i, rp], fv.at[i, 0], fp),
            copy("gm%d" % i, sm.at[i, rm], fv.at[i, 1], fm),
        ]

    def sD(i):
        got(st[i]["f2"])
        r = rows(f, 4 * G)
        s2[i] = (sm[i, r, :].astype(F32) + fv[i, 0].astype(F32) + fv[i, 1].astype(F32)).astype(BF)
        r = rows((s + 2) % 4, G)
        st[i]["s1"] = [
            copy("sp%d" % i, s2.at[i, r, L], sr.at[i, 0], sp),
            copy("sn%d" % i, s2.at[i, r, M], sr.at[i, 1], sn),
        ]

    def sE(i):
        got(st[i]["s1"])
        rp, rm = rows((s + 1) % 4, G), rows((s + 3) % 4, G)
        add_to(s2, i, rp, L, sr[i, 0])
        add_to(s2, i, rm, M, sr[i, 1])
        st[i]["s2"] = [
            copy("tp%d" % i, s2.at[i, rp], sv.at[i, 0], sp),
            copy("tn%d" % i, s2.at[i, rm], sv.at[i, 1], sn),
        ]

    def erow(f_, s_):
        return pl.ds(al(c * T + f_ * (4 * G) + s_ * G, G), G)

    def frow(f_):
        return pl.ds(al(c * T + f_ * (4 * G), 4 * G), 4 * G)

    def sF(i):
        got(st[i]["s2"])
        v = s2[i, rows(s, G), :].astype(F32) + sv[i, 0].astype(F32) + sv[i, 1].astype(F32)
        e = erow(f, s)
        which = (l + c) % 2
        target = tg[which, :, rows(chunk[i] % 4, K)].astype(F32)
        err[i, e, L] = (scale * (v[:, :K] - target)).astype(BF)
        err[i, e, M] = (scale * v[:, K:]).astype(BF)
        st[i]["a1"] = [
            copy("up%d" % i, err.at[i, e], err.at[i, e], sp),
            copy("un%d" % i, err.at[i, e], err.at[i, e], sn),
        ]

    def sG(i):
        got(st[i]["a1"])
        a, b = erow(f, (s + 3) % 4), erow(f, (s + 1) % 4)
        st[i]["a2"] = [
            copy("vp%d" % i, err.at[i, a, L], err.at[i, a, L], sp),
            copy("vn%d" % i, err.at[i, b, M], err.at[i, b, M], sn),
        ]

    def sH(i):
        got(st[i]["a2"])
        e = frow(f)
        st[i]["b1"] = [
            copy("wp%d" % i, err.at[i, e], err.at[i, e], fp),
            copy("wm%d" % i, err.at[i, e], err.at[i, e], fm),
        ]

    def sI(i):
        got(st[i]["b1"])
        a, b = frow((f + 3) % 4), frow((f + 1) % 4)
        st[i]["b2"] = [
            copy("qp%d" % i, err.at[i, a, L], err.at[i, a, L], fp),
            copy("qm%d" % i, err.at[i, b, M], err.at[i, b, M], fm),
        ]

    def sJ(i):
        got(st[i]["b2"])
        e = rows(c, T)
        st[i]["c2"] = copy("cb%d" % i, err.at[i, e], err.at[i, e], core)

    lo_of = [1 - l, l]
    xs = {}

    def blk(q, i, h):
        lo = lo_of[h]
        if q == 0:
            return lambda col: sm.at[i, pl.ds(0, R), pl.ds(al(lo * C + col * H, H), H)]
        r = wrow(chunk[i], lo)
        return lambda col: Wi.at[r, pl.ds(col * H, H)]

    def x_far(q, h):
        b = blk(q, 3, h)
        xs[q, h, "r"] = [
            send("xr%d%dp" % (q, h), b(1), xr.at[q, h, 0], xp),
            send("xr%d%dm" % (q, h), b(0), xr.at[q, h, 1], xm),
        ]

    def x_near(q, h):
        xs[q, h, "n"] = [
            send("xn%d%dp" % (q, h), blk(q, 1, h)(0), xv.at[q, h, 0, :, A], xp),
            send("xn%d%dm" % (q, h), blk(q, 2, h)(1), xv.at[q, h, 1, :, B], xm),
        ]

    def x_relay(q, h):
        got(xs[q, h, "r"])
        pair = ((blk(q, 1, h)(1), 0), (blk(q, 2, h)(0), 1))

        @pl.loop(0, R // 128)
        def _(j):
            r = rows(j, 128)
            for ref, n in pair:
                ref[r, :] = (ref[r, :].astype(F32) + xr[q, h, n, r, :].astype(F32)).astype(BF)

        xs[q, h, "v"] = [
            send("xv%d%dp" % (q, h), pair[0][0], xv.at[q, h, 0, :, B], xp),
            send("xv%d%dm" % (q, h), pair[1][0], xv.at[q, h, 1, :, A], xm),
        ]

    def x_final(q, h):
        got(xs[q, h, "n"])
        got(xs[q, h, "v"])
        b = blk(q, 0, h)
        base = 2 * (1 - q)

        @pl.loop(0, R // 128)
        def _(j):
            r = rows(j, 128)
            for col, o in ((0, base + 1), (1, base)):
                cc = pl.ds(col * H, H)
                v = b(col)[r, :].astype(F32) + xv[q, h, 0, r, cc].astype(F32) + xv[q, h, 1, r, cc].astype(F32)
                if h == 0:
                    ys[q, r, cc] = v.astype(BF)
                else:
                    stage[o, r, mine] = v.astype(BF)

        if h == 0:
            xs[q, "y"] = [
                send("y%dh" % q, ys.at[q, :, A], stage.at[base + 1, :, mine], mate),
                send("y%dg" % q, ys.at[q, :, B], stage.at[base, :, mine], mate),
            ]

    def sK(i, first):
        st[i]["c2"].wait_recv()
        for name in ("f1", "f2"):
            for cp in st[i][name]:
                cp.wait_send()
        for h in (0, 1):
            lo = lo_of[h]

            @pl.loop(0, R // 128)
            def _(j):
                fc = al(lo * R + j * 128, 128)
                e = err[i, :, pl.ds(fc, 128)]
                ed = err[i, :, pl.ds(al(K + fc, 128), 128)]
                g = dot_tn(e, ad[...])
                hv = g[:, :H] + dot_tn(ed, ad[:, B])
                r = rows(j, 128)
                sm[i, r, pl.ds(al(lo * C, H), H)] = hv.astype(BF)
                sm[i, r, pl.ds(al(lo * C + H, H), H)] = g[:, H:].astype(BF)

            if i == 3:
                x_far(0, h)
        if i == 2:
            x_near(0, 0)
            x_near(0, 1)
        w = rows(chunk[i] % 4, K)

        @pl.loop(0, 4)
        def _(j):
            r = rows(j, 256)
            v = dot_nn(err[i, r, L], Wo[w, :])
            t = dot_nn(err[i, r, M], Wo[w, A])
            if first:
                acc[r, A] = v[:, :H]
                acc[r, B] = v[:, H:] + t
            else:
                acc[r, A] = acc[r, A] + v[:, :H]
                acc[r, B] = acc[r, B] + v[:, H:] + t

    o2 = {}

    def xo2(which):
        if which == 0:
            got(o1o)
            o2[0] = ring2("o2o", Wo, l)
        else:
            got(o1t)
            o2[1] = ring2("o2t", Wo, 1 - l)

    sA(0); sB(0); xo2(0); sC(0); sD(0); xo2(1)
    sA(1); sA(2); sE(0); sB(1); sB(2)
    tg_loc.wait()
    tgx.wait_recv()
    sF(0); sC(1); sC(2); sG(0); sD(1); sD(2); sH(0)
    got(o2[0]); got(o2[1])
    sA(3); sE(1); sE(2); sI(0); sB(3); sF(1); sF(2); sJ(0); sC(3); sG(1); sG(2); sD(3); sH(1); sH(2)
    sK(0, True); sE(3); sI(1); sI(2); sF(3); sJ(1); sJ(2); sG(3); sK(1, False); sH(3); sK(2, False); sI(3); sJ(3); sK(3, False)

    x_relay(0, 0)

    @pl.loop(0, 8)
    def _(j):
        r = rows(j, 128)
        bg, bd = acc[r, A], acc[r, B]
        fd = fg[r, A]
        ad[r, A] = (bd * fd + bg * fg[r, B]).astype(BF)
        ad[r, B] = (bg * fd).astype(BF)

    def part_in(i, h):
        lo = lo_of[h]

        @pl.loop(0, R // 128)
        def _(j):
            fc = al((chunk[i] % 4) * K + lo * R + j * 128, 128)
            v = dot_tn(Tk[:, pl.ds(fc, 128)], ad[...])
            Wi[pl.ds(fc, 128), :] = v.astype(BF)

    for cp in i1o + i1t + i2o + i2t:
        cp.wait_send()
    pending[:] = [cp for cp in pending if not any(cp is o for o in i1o + i1t + i2o + i2t)]
    part_in(3, 0)
    x_relay(0, 1)
    x_far(1, 0)
    part_in(1, 0)
    part_in(2, 0)
    x_near(1, 0)
    x_final(0, 0)
    part_in(0, 0)
    part_in(3, 1)
    x_far(1, 1)
    x_relay(1, 0)
    part_in(1, 1)
    part_in(2, 1)
    x_near(1, 1)
    part_in(0, 1)
    x_final(0, 1)
    x_relay(1, 1)
    x_final(1, 0)
    got(xs[0, "y"])
    o_out = local(stage.at[pl.ds(2, 2)], out.at[pl.ds(2, 2)])
    x_final(1, 1)
    got(xs[1, "y"])
    o_in = local(stage.at[pl.ds(0, 2)], out.at[pl.ds(0, 2)])
    for cp in pending:
        cp.wait_send()
    for i in range(4):
        for name in ("s1", "s2", "a1", "a2", "b1", "b2"):
            for cp in st[i][name]:
                cp.wait_send()
        st[i]["c2"].wait_send()
        if i >= 2:
            st[i]["core"].wait_send()
    o_out.wait()
    o_in.wait()


def on_device(tokens, target, w_in, probe_in, w_out, probe_out):
    R, hid = w_in.shape
    T, D = tokens.shape
    groups = lax.axis_size("replica")
    H, K, C = hid // 2, 2 * R, hid
    scale = float(T * groups) ** (-0.5)
    V = pltpu.VMEM
    scratch = [
        V((2 * T, D), BF),
        V((D, C), BF),
        V((D, C), BF),
        V((2 * T, C), F32),
        V((2 * T, C), BF),
        V((2 * T, C), F32),
        V((2, T, 2 * K), BF),
        V((4, T, 2 * K), BF),
        V((4, 2, T // 4, K), BF),
        V((4, 2, T // 4, 2 * K), BF),
        V((4, T // 4, 2 * K), BF),
        V((4, 2, T // 16, K), BF),
        V((4, 2, T // 16, 2 * K), BF),
        V((4, 2 * T, 2 * K), BF),
        V((2, 2, 2, R, H), BF),
        V((2, 2, 2, R, C), BF),
        V((2, R, C), BF),
        V((4, R, C), BF),
        V((2, T // 16, D), BF),
        pltpu.SemaphoreType.DMA((8,)),
        pltpu.SemaphoreType.DMA((N_SEM,)),
        pltpu.SemaphoreType.DMA((N_SEM,)),
    ]
    res = pl.pallas_call(
        functools.partial(block_kernel, scale),
        out_shape=jax.ShapeDtypeStruct((4, R, hid), BF),
        in_specs=[pl.BlockSpec(memory_space=pl.ANY)] * 6,
        out_specs=pl.BlockSpec(memory_space=pl.ANY),
        scratch_shapes=scratch,
        compiler_params=pltpu.CompilerParams(collective_id=0, has_side_effects=True, vmem_limit_bytes=64 * 2**20),
        cost_estimate=pl.CostEstimate(flops=26 * T * D * hid, bytes_accessed=40 * 2**20, transcendentals=4 * T * H),
        name="sophia_block",
    )(tokens, target, w_in, probe_in, w_out, probe_out)
    res = res.astype(F32)
    grad_in, hv_in, grad_out, hv_out = res[0], res[1], res[2], res[3]
    hess_in = scale * probe_in.astype(F32) * hv_in
    hess_out = scale * probe_out.astype(F32) * hv_out
    return grad_in, hess_in, grad_out, hess_out


def solution(mesh):
    wide = P("replica", "shard")
    return jax.shard_map(
        on_device,
        mesh=mesh,
        in_specs=(P("replica", None), P("replica", None), wide, wide, wide, wide),
        out_specs=(wide, wide, wide, wide),
        check_vma=False,
    )
```

time: 1060 us -> 249 us (0.23)
  waiting for transfers between devices: 897 us -> 0 us
  Pallas kernels: 0 us -> 243 us
  matrix products: 65.5 us -> 0 us
  local copies, waits for them, and re-layouts: 62.4 us -> 1.57 us
  between operations: 14.3 us -> 0.68 us
  other arithmetic: 14.8 us -> 3.79 us
    all_gather x4 -> x0, waiting for transfers between devices: 391 us -> none  [the longest x1 102 us: on_device(): lax.all_gather(probe_in, 'replica', axis=0, tiled=True)]
    unnamed x9 -> x0, waiting for transfers between devices: 338 us -> none
    pallas_call x0 -> x1, Pallas kernels: none -> 243 us  [on_device(): pl.pallas_call(functools.partial(block_kernel, scale), out_shape=jax.Shap...]
    psum x1 -> x0, waiting for transfers between devices: 168 us -> none  [error_pair(): lax.psum(out_part.astype(jnp.bfloat16), 'shard').astype(jnp.float32)]
    dot_general x8 -> x0, matrix products: 65.5 us -> none  [the longest x3 26.6 us: inner_rows(): lax.dot_general(left, right, (((0,), (0,)), ((), ())), preferred_element_...]
    unnamed x45 -> x4, local copies, waits for them, and re-layouts: 50.5 us -> 0.01 us
  transfers between devices with their start and end apart: 7 -> 0, of which waited for: 7 -> 0; matrix products, arithmetic and copies ran while one was open for 6% -> 0% of each run, Pallas kernels for 0% -> 0%
where the time goes in v1:
time: 249 us
  Pallas kernels  243 us (98%)
  other arithmetic  3.79 us (2%)
    pallas_call x1, Pallas kernels, on_device(): pl.pallas_call(functools.partial(block_kernel, scale), out_shape=jax.Shap...  243 us

profile of v1, /device:TPU:1, one launch (start us, length us, event | category | flops | bytes accessed | tf_op | source)
XLA Modules:
  0.0 248.6 jit_solution(14702863387900290089)
XLA Ops:
  0.6 242.6 %sophia_block.1 = bf16[4,384,768]{2,1,0:T(8,128)(2,1)} custom-call(bf16[512,3072]{1,0:T(8,128)(2,1)} %tok.1, bf16[512,3072]{1,0:T(8,128)(2,1)} %tgt.1, bf16[384,768]{1,0:T(8,128)(2,1)} %w_in.1, bf16[384,768]{1,0:T(8,128)(2,1)} %p_in.1, bf16[384,768]{1,0:T(8,128)(2,1)} %w_out.1, bf16[384,768]{1,0:T(8,128)(2,1)} %p_out.1), custom_call_target="tpu_custom_call" | custom-call | flops 31406948352 | bytes 41943040 | tf_op jit(solution)/shard_map/sophia_block/pallas_call | solution.py:506
  243.2 0.0 copy-start
  243.3 0.0 copy-start.1
  243.3 2.2 convert_element_type.9
  245.4 0.0 copy-done
  245.4 0.0 copy-done.1
  245.4 1.6 fusion
  247.1 1.6 slice_bitcast_fusion.1
Async XLA Ops:
  243.2 2.2 copy-start
  243.3 2.2 copy-start.1
